TPU v7x, 512 devices: a whole 4x8x8 slice. The times are simulated.
512 devices in a mesh: sx: 16 (over z, core), sy: 4 (over x), mom: 8 (over y).
Axes of the slice: x: 4, y: 8, z: 8, core: 2. Of those that a mesh axis runs over, the one named last changes fastest.
Arguments:
- propagator: bfloat16 [2, 12, 12, 64, 6144], P(None, None, None, 'sx', 'sy'), may hold values from -2.6875 to 2.6875
- momenta: int32 [128, 3], P('mom'), may hold values from -4 to 4
- chan_moms: int32 [16, 2], replicated, may hold values from 0 to 127
- term_index: int32 [2, 16, 1536], P(None, 'mom', ('sx', 'sy')), may hold values from 0 to 1727
- term_weight: float32 [16, 1536], P('mom', ('sx', 'sy')), may hold values from -0.24 to 0.24
- lengths: int32 [16], P('mom'), may hold values from 1 to 1536, 8192 in all
Outputs:
- projected: float32 [128, 3456], P('mom', ('sx', 'sy'))
- correlator: float32 [2, 16], P(None, 'mom')
Inputs may be any that keep to these rules, and one draw needn't show every extreme that they name: The lengths of all 16 channels sum to 8192; the longest list has exactly 1536 live terms.
All inputs are finite; a program needn't handle non-finite values. No bound on the sum of `lengths` on one device may be relied on, other than what follows from the above.
Results may differ from a plain program's by a relative error of at most 0.0058.
Values sent between devices are 32-bit elements; how exact they have to be, the bound alone decides.
A program may use at most 64 MiB of HBM per device.

v0:
```python
import math

import jax
import jax.numpy as jnp
from jax import lax
from jax.sharding import PartitionSpec as P

LAT = 96


SPIN_SIGN = (-1.0, 1.0, -1.0, 1.0)
SPIN_FROM = (1, 0, 3, 2)
COLOUR_PAIRS = ((1, 2, 0), (2, 0, 1), (0, 1, 2))


def diquark_pairs(lift_real, lift_imag, prop_real, prop_imag, left_colour, right_colour):
    site_count = prop_real.shape[-1]
    row_span = lift_real.shape[2]
    total_real = jnp.zeros((row_span, 12, site_count), jnp.float32)
    total_imag = jnp.zeros((row_span, 12, site_count), jnp.float32)
    for spin_index in range(4):
        left_real = lift_real[left_colour, spin_index][:, None, :]
        left_imag = lift_imag[left_colour, spin_index][:, None, :]
        right_real = prop_real[right_colour, spin_index][None, :, :]
        right_imag = prop_imag[right_colour, spin_index][None, :, :]
        total_real = total_real + left_real * right_real - left_imag * right_imag
        total_imag = total_imag + left_real * right_imag + left_imag * right_real
    return (total_real, total_imag)


def baryon_rows(site_values, row_span):
    site_count = site_values.shape[-1]
    prop_real = site_values[0].reshape(3, 4, 12, site_count)
    prop_imag = site_values[1].reshape(3, 4, 12, site_count)
    lift_real = jnp.stack(
        [SPIN_SIGN[spin_index] * prop_real[:, SPIN_FROM[spin_index]] for spin_index in range(4)],
        axis=1,
    )
    lift_imag = jnp.stack(
        [SPIN_SIGN[spin_index] * prop_imag[:, SPIN_FROM[spin_index]] for spin_index in range(4)],
        axis=1,
    )
    block_real = jnp.zeros((row_span, 12, 12, site_count), jnp.float32)
    block_imag = jnp.zeros((row_span, 12, 12, site_count), jnp.float32)
    for left_colour, right_colour, third_colour in COLOUR_PAIRS:
        plus_real, plus_imag = diquark_pairs(
            lift_real, lift_imag, prop_real, prop_imag, left_colour, right_colour
        )
        minus_real, minus_imag = diquark_pairs(
            lift_real, lift_imag, prop_real, prop_imag, right_colour, left_colour
        )
        diquark_real = (plus_real - minus_real)[:, :, None, :]
        diquark_imag = (plus_imag - minus_imag)[:, :, None, :]
        quark_real = prop_real[third_colour, 0][None, None, :, :]
        quark_imag = prop_imag[third_colour, 0][None, None, :, :]
        block_real = block_real + diquark_real * quark_real - diquark_imag * quark_imag
        block_imag = block_imag + diquark_real * quark_imag + diquark_imag * quark_real
    return (
        block_real.reshape(row_span * 144, site_count),
        block_imag.reshape(row_span * 144, site_count),
    )


def phase_rows(momenta, coord_x, coord_y, coord_z):
    turns = (
        momenta[:, 0:1] * coord_x[None, :]
        + momenta[:, 1:2] * coord_y[None, :]
        + momenta[:, 2:3] * coord_z[None, :]
    ) % LAT
    angle = turns.astype(jnp.float32) * (2.0 * math.pi / LAT)
    return jnp.concatenate([jnp.cos(angle), jnp.sin(angle)], axis=0).astype(jnp.bfloat16)


def combine_parts(accumulated, mom_rows):
    half_width = accumulated.shape[1] // 2
    top_rows = accumulated[:mom_rows]
    bottom_rows = accumulated[mom_rows:]
    return jnp.concatenate(
        [
            top_rows[:, :half_width] + bottom_rows[:, half_width:],
            top_rows[:, half_width:] - bottom_rows[:, :half_width],
        ],
        axis=1,
    )


def correlate(first_rows, second_rows, left_index, right_index, live_weight):
    half_width = first_rows.shape[1] // 2
    left_real = jnp.take_along_axis(first_rows, left_index, axis=1)
    left_imag = jnp.take_along_axis(first_rows, left_index + half_width, axis=1)
    right_real = jnp.take_along_axis(second_rows, right_index, axis=1)
    right_imag = jnp.take_along_axis(second_rows, right_index + half_width, axis=1)
    corr_real = jnp.sum(live_weight * (left_real * right_real - left_imag * right_imag), axis=1)
    corr_imag = jnp.sum(live_weight * (left_real * right_imag + left_imag * right_real), axis=1)
    return jnp.stack([corr_real, corr_imag], axis=0)


def local(propagator, momenta, chan_moms, term_index, term_weight, lengths):
    row_count = propagator.shape[3]
    col_count = propagator.shape[4]
    y_rows = col_count // LAT
    space_devices = lax.axis_size("sx") * lax.axis_size("sy")
    owner_count = lax.axis_size("mom")
    volume = row_count * lax.axis_size("sx") * y_rows * lax.axis_size("sy") * LAT
    site_total = row_count * col_count
    block_size = math.gcd(site_total, 512)
    flat_prop = propagator.reshape(2, 12, 12, site_total)
    x_start = lax.axis_index("sx") * row_count
    y_start = lax.axis_index("sy") * y_rows
    mom_rows = momenta.shape[0]
    owner_index = lax.axis_index("mom")
    block_steps = jnp.arange(site_total // block_size, dtype=jnp.int32)

    def site_phases(moment_table, block_start):
        local_site = block_start + jnp.arange(block_size, dtype=jnp.int32)
        within = local_site % col_count
        coord_x = x_start + local_site // col_count
        return phase_rows(moment_table, coord_x, y_start + within // LAT, within % LAT)

    def add_block(running_sum, block_index):
        block_start = block_index * block_size
        site_values = lax.dynamic_slice_in_dim(flat_prop, block_start, block_size, 3).astype(
            jnp.float32
        )
        block_real, block_imag = baryon_rows(site_values, 12)
        block_values = jnp.concatenate([block_real, block_imag], axis=0).astype(jnp.bfloat16)
        phases = site_phases(momenta, block_start)
        product = lax.dot_general(
            phases, block_values, (((1,), (1,)), ((), ())), preferred_element_type=jnp.float32
        )
        return (running_sum + product, None)

    initial = jnp.zeros((2 * mom_rows, 3456), jnp.float32)
    accumulated, unused = lax.scan(add_block, initial, block_steps)
    combined = combine_parts(accumulated, mom_rows)
    own_blocks = lax.psum_scatter(combined, ("sx", "sy"), scatter_dimension=1, tiled=True) * (
        1.0 / math.sqrt(volume)
    )
    chan_own = lengths.shape[0]
    width_piece = own_blocks.shape[1]
    every_block = lax.all_gather(own_blocks[None], ("sx", "sy", "mom"), axis=0, tiled=True)
    every_block = every_block.reshape(space_devices, owner_count, mom_rows, width_piece)
    wanted = lax.dynamic_slice_in_dim(chan_moms, owner_index * chan_own, chan_own, 0).reshape(-1)
    picked = every_block[:, wanted // mom_rows, wanted % mom_rows, :]
    rows_full = picked.transpose(1, 0, 2).reshape(chan_own, 2, space_devices * width_piece)
    slot_count = term_weight.shape[1]
    slot_index = lax.axis_index(("sx", "sy")) * slot_count + jnp.arange(slot_count, dtype=jnp.int32)
    live_weight = jnp.where(slot_index[None, :] < lengths[:, None], term_weight, 0.0)
    partial_corr = correlate(
        rows_full[:, 0], rows_full[:, 1], term_index[0], term_index[1], live_weight
    )
    correlator = lax.psum(partial_corr, ("sx", "sy"))
    return (own_blocks, correlator)


def solution(mesh):
    in_specs = (
        P(None, None, None, "sx", "sy"),
        P("mom", None),
        P(),
        P(None, "mom", ("sx", "sy")),
        P("mom", ("sx", "sy")),
        P("mom"),
    )
    out_specs = (P("mom", ("sx", "sy")), P(None, "mom"))
    return jax.shard_map(local, mesh=mesh, in_specs=in_specs, out_specs=out_specs, check_vma=False)
```

profile of v0, /device:TPU:1, one launch (start us, length us, event | category | flops | bytes accessed | tf_op | source)
XLA Modules:
  0.0 705.7 jit_solution(12181628446086323750)
XLA Ops:
  7.3 6.6 reshape.670
  13.9 235.6 %while.14 = (s32[]{:T(128)}, f32[32,3456]{1,0:T(8,128)S(1)}, s32[16,3]{0,1:T(4,128)S(1)}, s32[]{:T(128)}, s32[12]{0:T(128)S(1)}, /*index=5*/s32[]{:T(128)}, bf16...) while((s32[]{:T(128)}, f32[32,3456]{1,0:T(8,128)S(1)}, ...), condition=%wide.region_1.2_spmd.clone, body=%wide.region_0.1_spmd.clone.sunk | while | flops 155920384 | bytes 26768132 | solution.py:134
  19.4 4.8 subtract_convert_fusion.2
  24.2 3.9 reshape.676
  39.1 4.8 subtract_convert_fusion.2
  43.8 3.9 reshape.676
  49.9 3.2 convolution_add_fusion.2
  58.7 4.8 subtract_convert_fusion.2
  63.5 3.9 reshape.676
  78.4 4.8 subtract_convert_fusion.2
  83.1 3.9 reshape.676
  89.2 3.2 convolution_add_fusion.2
  98.0 4.8 subtract_convert_fusion.2
  102.8 3.9 reshape.676
  117.6 4.8 subtract_convert_fusion.2
  122.4 3.9 reshape.676
  137.3 4.8 subtract_convert_fusion.2
  142.0 3.9 reshape.676
  156.9 4.8 subtract_convert_fusion.2
  161.7 3.9 reshape.676
  176.5 4.8 subtract_convert_fusion.2
  181.3 3.9 reshape.676
  196.2 4.8 subtract_convert_fusion.2
  200.9 3.9 reshape.676
  215.8 4.8 subtract_convert_fusion.2
  220.6 3.9 reshape.676
  235.5 4.8 subtract_convert_fusion.2
  240.2 3.9 reshape.676
  252.4 187.6 %all-reduce.3.cloned.1.call-done = f32[16,3456]{1,0:T(8,128)} async-done(((f32[16,3456]{1,0:T(8,128)}), f32[16,3456]{1,0:T(8,128)}) %all-reduce.3.cloned.1.call-update) | async-done | bytes 221200
  442.1 119.7 %all-gather.3.cloned.1.call-done = f32[8192,54]{1,0:T(8,128)} async-done(((f32[16,54]{1,0:T(8,128)}), f32[8192,54]{1,0:T(8,128)}) %all-gather.3.cloned.1.call-update) | async-done | bytes 1769488 | tf_op jit(solution)/shard_map/all_gather | solution.py:141
  561.8 5.7 copy.25
  575.3 123.5 %psum.7 = f32[2,2]{1,0:T(2,128)} all-reduce(f32[2,2]{1,0:T(2,128)S(1)} %pad_maximum_fusion.1), channel_id=1, replica_groups=mesh['sx'=16,'sy'=4,'mom'=8] {'sx','sy'}, use_global_device_ids=true, to_apply=%region_5.7 | all-reduce | flops 4 | bytes 32 | tf_op jit(solution)/shard_map/psum | solution.py:152
  (295 shorter events, 129.4 us)
Async XLA Ops:
  7.2 434.3 %copy-start = (s32[16,2]{0,1:T(2,128)S(1)}, s32[16,2]{0,1:T(2,128)}, u32[]{:S(2)}) copy-start(s32[16,2]{0,1:T(2,128)} %param.12) | copy-start | bytes 388
  7.2 6.7 copy-start.1
  7.2 432.9 %all-reduce.3.cloned.1.call-start = ((), (), s32[]{:S(2)}) async-start(), calls=%async_computation.1 | async-start | bytes 442368
  13.9 427.9 %copy-start.2 = (s32[2,2,24]{2,1,0:T(2,128)S(1)}, s32[2,2,24]{2,1,0:T(2,128)}, u32[]{:S(2)}) copy-start(s32[2,2,24]{2,1,0:T(2,128)} %param.13) | copy-start | bytes 1156
  250.5 311.3 %all-gather.3.cloned.1.call-start = ((), (), s32[]{:S(2)}) async-start(), calls=%async_computation | async-start | bytes 4202496 | tf_op jit(solution)/shard_map/all_gather | solution.py:141
  561.8 13.3 %copy-start.3 = (f32[2,24]{1,0:T(2,128)S(1)}, f32[2,24]{1,0:T(2,128)}, u32[]{:S(2)}) copy-start(f32[2,24]{1,0:T(2,128)} %param.14) | copy-start | bytes 580
  561.8 13.3 %copy-start.4 = (s32[2]{0:T(128)S(1)}, s32[2]{0:T(128)}, u32[]{:S(2)}) copy-start(s32[2]{0:T(128)} %param.15) | copy-start | bytes 28
Sparse Core Ops, SparseCore 0:
  250.6 189.4 all-reduce.2
  445.6 116.1 all-gather.2
where the time goes:
time: 711 us; the launch traced here: 706 us
  waiting for transfers between devices  307 us (43%)
  blocking collectives  123 us (17%)
  other arithmetic  114 us (16%)
  local copies, waits for them, and re-layouts  99.8 us (14%)
  matrix products  38.3 us (5%)
  between operations  14.8 us (2%)
  loops' own time  8.1 us (1%)
    unnamed x3, waiting for transfers between devices  188 us
    psum x1, blocking collectives, local(): correlator = lax.psum(partial_corr, ('sx', 'sy'))  123 us
    all_gather x1, waiting for transfers between devices, local(): lax.all_gather(own_blocks[None], ('sx', 'sy', 'mom'), axis=0, tiled=True)  120 us
    another operation x24, local copies, waits for them, and re-layouts  69.6 us
    another operation x24, other arithmetic  59.9 us
    dot_general x12, matrix products, add_block(): lax.dot_general(phases, block_values, (((1,), (1,)), ((), ())), preferred...  38.3 us
    sub x36, other arithmetic, baryon_rows(): diquark_real = (plus_real - minus_real)[:, :, None, :]  18.7 us
    sub x36, other arithmetic, baryon_rows(): diquark_imag = (plus_imag - minus_imag)[:, :, None, :]  18.7 us
  transfers between devices with their start and end apart: 2, of which 2 were waited for; matrix products, arithmetic and copies ran while one was open for 0% of the time, Pallas kernels for 0%

commit v1 on v0

v1 whole, which is shorter than its diff:
```python
import math
import jax
import jax.numpy as jnp
from jax import lax
from jax.experimental import pallas as pl
from jax.experimental.pallas import tpu as pltpu
from jax.sharding import PartitionSpec as P

LAT = 96
PAIRS = 10
SCALE = 1.0 / math.sqrt(393216)
COLOURS = ((1, 2, 0), (2, 0, 1), (0, 1, 2))


def sine(turns):
    u = turns - 96.0 * jnp.floor(turns * (1.0 / 96.0) + 0.5)
    v = jnp.where(u > 24.0, 48.0 - u, jnp.where(u < -24.0, -48.0 - u, u))
    x = v * (2.0 * math.pi / 96.0)
    y = x * x
    r = jnp.float32(1.0 / 6227020800.0)
    for c in (-1.0 / 39916800.0, 1.0 / 362880.0, -1.0 / 5040.0, 1.0 / 120.0, -1.0 / 6.0, 1.0):
        r = r * y + c
    return x * r


def cosine(turns):
    return sine(turns + 24.0)


def cmul(a, b):
    return (a[0] * b[0] - a[1] * b[1], a[0] * b[1] + a[1] * b[0])


def cadd(a, b):
    return (a[0] + b[0], a[1] + b[1])


def csub(a, b):
    return (a[0] - b[0], a[1] - b[1])


def start_loads(s_hbm, buf, sem):
    for t in range(3):
        for c in range(4 * t, 4 * t + 4):
            pltpu.make_async_copy(
                s_hbm.at[:, :, :, :, pl.ds(128 * c, 128)], buf.at[:, :, :, c], sem.at[t]
            ).start()


def wait_load(buf, sem, t):
    part = buf.at[:, :, :, 4 * t : 4 * t + 4]
    pltpu.make_async_copy(part, part, sem.at[t]).wait()


def fill_phases(mom, rhs, tab):
    x3 = lax.broadcasted_iota(jnp.int32, (96, 128), 0).astype(jnp.float32)
    c3 = cosine(mom[2:3] * x3)
    s3 = sine(mom[2:3] * x3)
    x2 = lax.broadcasted_iota(jnp.int32, (16, 128), 0).astype(jnp.float32)
    tab[0] = cosine(mom[1:2] * x2)
    tab[1] = sine(mom[1:2] * x2)

    def row(b, _):
        c2 = tab[0, pl.ds(b, 1), :]
        s2 = tab[1, pl.ds(b, 1), :]
        at = pl.ds(pl.multiple_of(96 * b, 96), 96)
        rhs[at, 0:128] = (c2 * c3 - s2 * s3).astype(jnp.bfloat16)
        rhs[at, 128:256] = (s2 * c3 + c2 * s3).astype(jnp.bfloat16)
        return 0

    lax.fori_loop(0, 16, row, 0)


def blocks(t, y, buf, sem, skp, lhs):
    low = lax.broadcasted_iota(jnp.int32, (8, 128), 0) < 4

    def rot(v):
        return pltpu.roll(v, 4, 0)

    def load(part, row, i):
        return buf[part, row, i, 4 * t : 4 * t + 4].reshape(16, 128).astype(jnp.float32)

    def pack_k(kp, _):
        for part in range(2):
            for c in range(3):
                a = load(part, 4 * c, 2 * kp)
                b = load(part, 4 * c, 2 * kp + 1)
                for h in range(2):
                    ah, bh = a[8 * h : 8 * h + 8], b[8 * h : 8 * h + 8]
                    skp[2 * h, part, c, kp] = jnp.where(low, ah, rot(bh))
                    skp[2 * h + 1, part, c, kp] = jnp.where(low, rot(ah), bh)
        return 0

    def spins(colour, idx):
        return [(load(0, 4 * colour + s, idx), load(1, 4 * colour + s, idx)) for s in range(4)]

    def pair(p, _):
        e = PAIRS * y + p
        d = e // 12
        i = e - 12 * d
        j = lax.rem(i + d, 12)
        q = []
        for a, b, c in COLOURS:
            A, B, A2, B2 = spins(a, i), spins(b, j), spins(a, j), spins(b, i)
            total = None
            for s, u in ((0, 1), (2, 3)):
                term = csub(cmul(A[s], B[u]), cmul(A[u], B[s]))
                term = cadd(term, csub(cmul(A2[s], B2[u]), cmul(A2[u], B2[s])))
                total = term if total is None else cadd(total, term)
            q.append((c, total))
        for ch in range(4):
            h, odd = ch // 2, ch % 2
            dup = {}
            for c, total in q:
                both = []
                for v in total:
                    v = v[8 * h : 8 * h + 8]
                    r = rot(v)
                    both.append(jnp.where(low, r, v) if odd else jnp.where(low, v, r))
                dup[c] = tuple(both)
            for kq in range(3):
                halves = []
                for kp in (2 * kq, 2 * kq + 1):
                    tot = None
                    for c in range(3):
                        prod = cmul(dup[c], (skp[ch, 0, c, kp], skp[ch, 1, c, kp]))
                        tot = prod if tot is None else cadd(tot, prod)
                    halves.append(tot)
                for part in range(2):
                    rows = pl.ds(pl.multiple_of(96 * p + 48 * part + 16 * kq, 16), 16)
                    lanes = slice(512 * t + 128 * ch, 512 * t + 128 * ch + 128)
                    lhs[rows, lanes] = jnp.concatenate(
                        [halves[0][part], halves[1][part]], axis=0
                    ).astype(jnp.bfloat16)
        return 0

    wait_load(buf, sem, t)
    lax.fori_loop(0, 6, pack_k, 0)
    lax.fori_loop(0, PAIRS, pair, 0)


def finish(mom, x0, y0, scale, chan, acc, zbuf, part1):
    x1 = lax.broadcasted_iota(jnp.int32, (8, 128), 0) % 4 + x0
    turns = mom[0:1] * x1.astype(jnp.float32) + mom[1:2] * y0.astype(jnp.float32)
    fc, fs = cosine(turns) * scale, sine(turns) * scale

    def pair(p, _):
        for g in range(6):
            r = acc[pl.ds(pl.multiple_of(96 * p + 8 * g, 8), 8), :]
            m = acc[pl.ds(pl.multiple_of(96 * p + 48 + 8 * g, 8), 8), :]
            re = r[:, :128] + m[:, 128:]
            im = m[:, :128] - r[:, 128:]
            at = pl.ds(pl.multiple_of(48 * p + 8 * g, 8), 8)
            zbuf[0, at, :] = fc * re + fs * im
            zbuf[1, at, :] = fc * im - fs * re
        return 0

    lax.fori_loop(0, PAIRS, pair, 0)
    zbuf[:, 480:512, :] = jnp.zeros((2, 32, 128), jnp.float32)
    for part in range(2):
        tot = zbuf[part, pl.ds(0, 128, stride=4), :]
        for k in range(1, 4):
            tot = tot + zbuf[part, pl.ds(k, 128, stride=4), :]
        turned = tot.T
        for g in range(8):
            part1[g, 16 * part : 16 * part + 16, :] = turned[16 * g : 16 * g + 16]
    for g in range(8):
        for k in range(4):
            n = chan[2 * g + k // 2, k % 2]
            for part in range(2):
                row = part1[pl.ds(n // 16, 1), pl.ds(16 * part + n % 16, 1), :]
                at = 32 + 2 * k + part
                part1[g : g + 1, at : at + 1, :] = row


def place(m):
    i = jnp.floor((m + 0.5) * (1.0 / 144.0))
    r = m - 144.0 * i
    j = jnp.floor((r + 0.5) * (1.0 / 12.0))
    k = r - 12.0 * j
    d = j - i
    d = jnp.where(d < 0.0, d + 12.0, d)
    flip = (d > 6.0) | ((d == 6.0) & (i >= 6.0))
    e = jnp.where(flip, 12.0 * (12.0 - d) + j, 12.0 * d + i)
    slot = jnp.floor((e + 0.5) * (1.0 / PAIRS))
    return slot, (e - PAIRS * slot) * 12.0 + k


def pick(x, lane):
    return jnp.take_along_axis(x, lane, axis=1, mode="promise_in_bounds")


def kernel(
    s_hbm, momenta, chan, tindex, tweight, lengths, out, corr,
    buf, rhs, tab, skp, lhs, acc, zbuf,
    mom_box, term_box, term_all, part1, got1, part2, got2, part3, got3,
    chan4, rows4, gotc, goto, load_sem, send_sem, recv_sem,
):
    sx, x, y = lax.axis_index("sx"), lax.axis_index("sy"), lax.axis_index("mom")
    z, core = sx // 2, lax.rem(sx, 2)
    b = 4 * core + x

    def b_dev(g):
        return (2 * z + g // 4, lax.rem(g, 4), y)

    def z_dev(g):
        return (2 * g + core, x, y)

    def y_dev(g):
        return (sx, x, g)

    def step(v, o):
        return lax.rem(v + o, 8)

    def copy(src, dst, stage, o, dev):
        return pltpu.make_async_remote_copy(
            src_ref=src, dst_ref=dst, send_sem=send_sem.at[stage, o],
            recv_sem=recv_sem.at[stage, o], device_id=dev,
            device_id_type=pl.DeviceIdType.MESH,
        )

    start_loads(s_hbm, buf, load_sem)
    barrier = pltpu.get_barrier_semaphore()
    for o in range(1, 8):
        for dev in (b_dev(step(b, o)), z_dev(step(z, o)), y_dev(step(y, o))):
            pl.semaphore_signal(
                barrier, inc=1, device_id=dev, device_id_type=pl.DeviceIdType.MESH
            )
        pl.semaphore_signal(
            barrier, inc=1, device_id=(2 * z + y // 4, lax.rem(y, 4), step(y, o)),
            device_id_type=pl.DeviceIdType.MESH,
        )
    alone = b == y

    @pl.when(jnp.logical_not(alone))
    def _():
        pl.semaphore_signal(
            barrier, inc=1, device_id=(2 * z + y // 4, lax.rem(y, 4), y),
            device_id_type=pl.DeviceIdType.MESH,
        )

    blocks(0, y, buf, load_sem, skp, lhs)

    rows = lax.broadcasted_iota(jnp.int32, (8, 128), 0)
    lanes = lax.broadcasted_iota(jnp.int32, (8, 128), 1)
    tile = jnp.zeros((8, 128), jnp.float32)
    for n in range(16):
        here = lanes == 16 * y + n
        for k in range(3):
            tile = jnp.where(here & (rows == k), momenta[n, k].astype(jnp.float32), tile)
    mom_box[0] = tile

    term_box[0] = jnp.zeros((8, 128), jnp.float32)
    live = lax.broadcasted_iota(jnp.int32, (2, 24), 1) + (8 * z + b) * 24
    owner = lax.broadcasted_iota(jnp.int32, (2, 24), 0)
    size = jnp.where(owner == 0, lengths[0], lengths[1])
    for side in range(2):
        slot, lane = place(tindex[side].astype(jnp.float32))
        term_box[0, 2 * side : 2 * side + 2, 0:24] = slot * 128.0 + lane
    term_box[0, 4:6, 0:24] = jnp.where(live < size, tweight[...], 0.0)
    term_box[0] = pltpu.roll(term_box[0], 32 * lax.rem(b, 4), 1)

    pl.semaphore_wait(barrier, jnp.where(alone, 28, 29))
    sent = []
    for o in range(1, 8):
        c = copy(mom_box.at[0], mom_box.at[o], 0, o, y_dev(step(y, o)))
        c.start()
        sent.append(c)
    boxes = []
    for o in range(1, 8):
        c = copy(term_box.at[0], term_box.at[o], 1, o, b_dev(step(b, o)))
        c.start()
        boxes.append(c)

    blocks(1, y, buf, load_sem, skp, lhs)

    for c in sent:
        c.wait_recv()
    mom = mom_box[0]
    for o in range(1, 8):
        mom = mom + mom_box[o]
    for c in boxes:
        c.wait_recv()
    for half in range(2):
        joined = jnp.zeros((8, 128), jnp.float32)
        for o in range(8):
            source = lax.rem(b + 8 - o, 8)
            joined = joined + jnp.where(source // 4 == half, term_box[o], 0.0)
        term_all[z, half] = joined
    sent += boxes
    boxes = []
    for o in range(1, 8):
        c = copy(term_all.at[z], term_all.at[z], 2, o, z_dev(step(z, o)))
        c.start()
        boxes.append(c)

    blocks(2, y, buf, load_sem, skp, lhs)
    fill_phases(mom, rhs, tab)
    acc[...] = jnp.dot(lhs[...], rhs[...], preferred_element_type=jnp.float32)
    finish(mom, 4 * sx, 16 * x, SCALE, chan, acc, zbuf, part1)

    hops = []
    for o in range(1, 8):
        g = step(b, o)
        c = copy(part1.at[g], got1.at[o], 3, o, b_dev(g))
        c.start()
        hops.append(c)
    total = part1[b]
    for c in hops:
        c.wait_recv()
    for o in range(1, 8):
        total = total + got1[o]
    sent += hops
    got1[0] = total
    for g in range(8):
        part2[g, 0:2] = got1[0, 2 * g : 2 * g + 2]
        part2[g, 2:4] = got1[0, 16 + 2 * g : 18 + 2 * g]
        part2[g, 4:5] = got1[0, 32 + g : 33 + g]
        part2[g, 5:8] = jnp.zeros((3, 128), jnp.float32)

    hops = []
    for o in range(1, 8):
        g = step(z, o)
        c = copy(part2.at[g], got2.at[o], 4, o, z_dev(g))
        c.start()
        hops.append(c)
    total = part2[z]
    for c in hops:
        c.wait_recv()
    for o in range(1, 8):
        total = total + got2[o]
    sent += hops
    part3[...] = total

    def third(o, slot):
        g = step(b, o)
        return pltpu.make_async_remote_copy(
            src_ref=part3, dst_ref=got3.at[slot], send_sem=send_sem.at[5, o],
            recv_sem=recv_sem.at[5, slot], device_id=(2 * z + g // 4, lax.rem(g, 4), b),
            device_id_type=pl.DeviceIdType.MESH,
        )

    for o in range(1, 8):
        third(o, y).start()

    @pl.when(jnp.logical_not(alone))
    def _():
        third(0, y).start()

    @pl.when(alone)
    def _():
        got3[y] = part3[...]

    for k in range(8):
        @pl.when(jnp.logical_not(alone & (y == k)))
        def _():
            third(0, k).wait_recv()

    column = (lanes + 54 * (8 * lax.rem(rows, 4) + b)).astype(jnp.float32)
    slot, lane = place(column)
    lane = lane.astype(jnp.int32)
    first = rows < 4
    news = [jnp.zeros((8, 128), jnp.float32), jnp.zeros((8, 128), jnp.float32)]
    for k in range(8):
        have = got3[k]
        for n in range(2):
            real = jnp.broadcast_to(have[n : n + 1], (8, 128))
            imag = jnp.broadcast_to(have[n + 2 : n + 3], (8, 128))
            value = pick(jnp.where(first, real, imag), lane)
            news[n] = jnp.where(slot == k, value, news[n])
    for g in range(8):
        for n in range(2):
            rows4[g, n : n + 1] = news[n][g : g + 1]
    chan4[...] = got3[:, 4, :]
    gotc[z] = chan4[...]
    goto[z] = rows4[z]

    hops = []
    for o in range(1, 8):
        g = step(z, o)
        c = copy(chan4, gotc.at[z], 6, o, z_dev(g))
        c.start()
        hops.append(c)
        c = copy(rows4.at[g], goto.at[z], 7, o, z_dev(g))
        c.start()
        hops.append(c)
    for c in boxes:
        c.wait_recv()
    sent += boxes
    terms = [term_all[:, :, k, :].reshape(16, 128) for k in range(6)]
    for c in hops:
        c.wait_recv()
    sent += hops
    answer = jnp.zeros((2, 2), jnp.float32)
    at_row = lax.broadcasted_iota(jnp.int32, (2, 2), 0)
    at_col = lax.broadcasted_iota(jnp.int32, (2, 2), 1)
    for h in range(2):
        sides = []
        for side in range(2):
            slot = jnp.floor((terms[2 * side + h] + 0.5) * (1.0 / 128.0))
            lane = (terms[2 * side + h] - 128.0 * slot).astype(jnp.int32)
            both = []
            for part in range(2):
                table = gotc[4 * h + 2 * side + part]
                chosen = []
                for u in range(2):
                    value = jnp.zeros((8, 128), jnp.float32)
                    for k in range(8):
                        have = pick(
                            jnp.broadcast_to(table[k : k + 1], (8, 128)), lane[8 * u : 8 * u + 8]
                        )
                        value = jnp.where(slot[8 * u : 8 * u + 8] == k, have, value)
                    chosen.append(value)
                both.append(jnp.concatenate(chosen, axis=0))
            sides.append(tuple(both))
        prod = cmul(sides[0], sides[1])
        for part in range(2):
            answer = jnp.where(
                (at_row == part) & (at_col == h), jnp.sum(terms[4 + h] * prod[part]), answer
            )
    corr[...] = answer
    out[...] = goto[...].reshape(16, 128)[:, :54]

    for c in sent:
        c.wait_send()
    for o in range(1, 8):
        third(o, y).wait_send()

    @pl.when(jnp.logical_not(alone))
    def _():
        third(0, y).wait_send()


def local(propagator, momenta, chan_moms, term_index, term_weight, lengths):
    f32 = jnp.float32
    vmem = pl.BlockSpec(memory_space=pltpu.VMEM)
    smem = pl.BlockSpec(memory_space=pltpu.SMEM)
    return pl.pallas_call(
        kernel,
        out_shape=(
            jax.ShapeDtypeStruct((16, 54), f32),
            jax.ShapeDtypeStruct((2, 2), f32),
        ),
        in_specs=[pl.BlockSpec(memory_space=pl.ANY), smem, smem, vmem, vmem, smem],
        out_specs=(vmem, vmem),
        scratch_shapes=[
            pltpu.VMEM((2, 12, 12, 12, 4, 128), jnp.bfloat16),
            pltpu.VMEM((1536, 256), jnp.bfloat16),
            pltpu.VMEM((2, 16, 128), f32),
            pltpu.VMEM((4, 2, 3, 6, 8, 128), f32),
            pltpu.VMEM((96 * PAIRS, 1536), jnp.bfloat16),
            pltpu.VMEM((96 * PAIRS, 256), f32),
            pltpu.VMEM((2, 512, 128), f32),
            pltpu.VMEM((8, 8, 128), f32),
            pltpu.VMEM((8, 8, 128), f32),
            pltpu.VMEM((8, 2, 8, 128), f32),
            pltpu.VMEM((8, 40, 128), f32),
            pltpu.VMEM((8, 40, 128), f32),
            pltpu.VMEM((8, 8, 128), f32),
            pltpu.VMEM((8, 8, 128), f32),
            pltpu.VMEM((8, 128), f32),
            pltpu.VMEM((8, 8, 128), f32),
            pltpu.VMEM((8, 128), f32),
            pltpu.VMEM((8, 2, 128), f32),
            pltpu.VMEM((8, 8, 128), f32),
            pltpu.VMEM((8, 2, 128), f32),
            pltpu.SemaphoreType.DMA((3,)),
            pltpu.SemaphoreType.DMA((8, 8)),
            pltpu.SemaphoreType.DMA((8, 8)),
        ],
        compiler_params=pltpu.CompilerParams(
            collective_id=0, has_side_effects=True, vmem_limit_bytes=40 * 2**20
        ),
    )(propagator, momenta, chan_moms, term_index, term_weight, lengths)


def solution(mesh):
    in_specs = (
        P(None, None, None, "sx", "sy"),
        P("mom", None),
        P(),
        P(None, "mom", ("sx", "sy")),
        P("mom", ("sx", "sy")),
        P("mom"),
    )
    out_specs = (P("mom", ("sx", "sy")), P(None, "mom"))
    return jax.shard_map(local, mesh=mesh, in_specs=in_specs, out_specs=out_specs, check_vma=False)
```

time: 711 us -> 53.4 us (0.08)
  waiting for transfers between devices: 307 us -> 0 us
  blocking collectives: 123 us -> 0 us
  other arithmetic: 114 us -> 0 us
  local copies, waits for them, and re-layouts: 99.8 us -> 6.69 us
  Pallas kernels: 0 us -> 45.8 us
  matrix products: 38.3 us -> 0 us
  between operations: 14.8 us -> 0.64 us
  loops' own time: 8.1 us -> 0 us
    unnamed x3 -> x0, waiting for transfers between devices: 188 us -> none
    psum x1 -> x0, blocking collectives: 123 us -> none  [local(): correlator = lax.psum(partial_corr, ('sx', 'sy'))]
    all_gather x1 -> x0, waiting for transfers between devices: 120 us -> none  [local(): lax.all_gather(own_blocks[None], ('sx', 'sy', 'mom'), axis=0, tiled=True)]
    another operation x24 -> x0, local copies, waits for them, and re-layouts: 69.6 us -> none
    another operation x25 -> x0, other arithmetic: 59.9 us -> none
    pallas_call x0 -> x1, Pallas kernels: none -> 45.8 us  [local(): pl.pallas_call(kernel, out_shape=(jax.ShapeDtypeStruct((16, 54), f32), ja...]
    dot_general x12 -> x0, matrix products: 38.3 us -> none  [add_block(): lax.dot_general(phases, block_values, (((1,), (1,)), ((), ())), preferred...]
    sub x72 -> x0, other arithmetic: 37.4 us -> none  [the longest x36 18.7 us: baryon_rows(): diquark_real = (plus_real - minus_real)[:, :, None, :]]
  transfers between devices with their start and end apart: 2 -> 0, of which waited for: 2 -> 0; matrix products, arithmetic and copies ran while one was open for 0% -> 0% of each run, Pallas kernels for 0% -> 0%
where the time goes in v1:
time: 53.4 us; the launch traced here: 53.2 us
  Pallas kernels  45.8 us (86%)
  local copies, waits for them, and re-layouts  6.69 us (13%)
  between operations  0.64 us (1%)
    pallas_call x1, Pallas kernels, local(): pl.pallas_call(kernel, out_shape=(jax.ShapeDtypeStruct((16, 54), f32), ja...  45.8 us
    unnamed x12, local copies, waits for them, and re-layouts  6.69 us

profile of v1, /device:TPU:1, one launch (start us, length us, event | category | flops | bytes accessed | tf_op | source)
XLA Modules:
  0.0 53.2 jit_solution(5888877932987998979)
XLA Ops:
  0.6 0.8 %copy.8.momenta = s32[16,3]{1,0:T(8,128)S(1)} copy(s32[16,3]{0,1:T(4,128)} %param.7) | data formatting | bytes 384 | tf_op args[1]
  1.4 0.8 %copy.9.chan = s32[16,2]{1,0:T(8,128)S(1)} copy(s32[16,2]{0,1:T(2,128)} %param.8) | data formatting | bytes 256 | tf_op args[2]
  2.1 0.0 copy-start
  2.1 2.0 %copy-done = bf16[2,12,12,4,1536]{4,3,2,1,0:T(4,128)(2,1)S(1)} copy-done((bf16[2,12,12,4,1536]{4,3,2,1,0:T(4,128)(2,1)S(1)}, bf16[2,12,12,4,1536]{4,3,2,1,0:T(4,128)(2,1)}, u32[]{:S(2)}) %copy-start) | copy-done | bytes 3538968
  4.1 0.0 copy-start.1
  4.1 0.7 %copy-done.1 = s32[2,2,24]{2,1,0:T(2,128)S(1)} copy-done((s32[2,2,24]{2,1,0:T(2,128)S(1)}, s32[2,2,24]{2,1,0:T(2,128)}, u32[]{:S(2)}) %copy-start.1) | copy-done | bytes 408
  4.8 0.0 copy-start.2
  4.8 0.7 %copy-done.2 = f32[2,24]{1,0:T(2,128)S(1)} copy-done((f32[2,24]{1,0:T(2,128)S(1)}, f32[2,24]{1,0:T(2,128)}, u32[]{:S(2)}) %copy-start.2) | copy-done | bytes 216
  5.5 0.0 copy-start.3
  5.5 0.7 %copy-done.3 = s32[2]{0:T(128)S(1)} copy-done((s32[2]{0:T(128)S(1)}, s32[2]{0:T(128)}, u32[]{:S(2)}) %copy-start.3) | copy-done | bytes 32
  6.2 45.8 %shard_map.77 = (f32[16,54]{1,0:T(8,128)S(1)}, f32[2,2]{1,0:T(2,128)S(1)}) custom-call(bf16[2,12,12,4,1536]{4,3,2,1,0:T(4,128)(2,1)S(1)} %copy-done, s32[16,3]{1,0:T(8,128)S(1)} %copy.8.momenta, s32[16,2]{1,0:T(8,128)S(1)} %copy.9.chan, s32[2,2,24]{2,1,0:T(2,128)S(1)} %copy-done.1, f32[2,24]{1,0:T(2,128)S(1)} %copy-done.2, s32[2]{0:T(128)S(1)} %copy-done.3), custom_call_target="tpu_custom_call" | custom-call | tf_op jit(solution)/shard_map/pallas_call | solution.py:438
  52.0 0.6 %copy.12 = f32[16,54]{1,0:T(8,128)} copy(f32[16,54]{1,0:T(8,128)S(1)} %get-tuple-element.4) | data formatting | bytes 6912
  52.6 0.6 %copy.13 = f32[2,2]{1,0:T(2,128)} copy(f32[2,2]{1,0:T(2,128)S(1)} %get-tuple-element.5) | data formatting | bytes 32
Async XLA Ops:
  2.1 2.0 %copy-start = (bf16[2,12,12,4,1536]{4,3,2,1,0:T(4,128)(2,1)S(1)}, bf16[2,12,12,4,1536]{4,3,2,1,0:T(4,128)(2,1)}, u32[]{:S(2)}) copy-start(bf16[2,12,12,4,1536]{4,3,2,1,0:T(4,128)(2,1)} %s_hbm.1) | copy-start | bytes 10616836
  4.1 0.7 %copy-start.1 = (s32[2,2,24]{2,1,0:T(2,128)S(1)}, s32[2,2,24]{2,1,0:T(2,128)}, u32[]{:S(2)}) copy-start(s32[2,2,24]{2,1,0:T(2,128)} %tindex.1) | copy-start | bytes 1156
  4.8 0.7 %copy-start.2 = (f32[2,24]{1,0:T(2,128)S(1)}, f32[2,24]{1,0:T(2,128)}, u32[]{:S(2)}) copy-start(f32[2,24]{1,0:T(2,128)} %tweight.1) | copy-start | bytes 580
  5.5 0.7 %copy-start.3 = (s32[2]{0:T(128)S(1)}, s32[2]{0:T(128)}, u32[]{:S(2)}) copy-start(s32[2]{0:T(128)} %lengths.1) | copy-start | bytes 28

commit v2 on v1

v2 whole, which is shorter than its diff:
```python
import math
import jax
import jax.numpy as jnp
from jax import lax
from jax.experimental import pallas as pl
from jax.experimental.pallas import tpu as pltpu
from jax.sharding import PartitionSpec as P

LAT = 96
PAIRS = 10
SCALE = 1.0 / math.sqrt(393216)
IM = 24
COLOURS = ((1, 2, 0), (2, 0, 1), (0, 1, 2))


def sine(turns):
    u = turns - 96.0 * jnp.floor(turns * (1.0 / 96.0) + 0.5)
    v = jnp.where(u > 24.0, 48.0 - u, jnp.where(u < -24.0, -48.0 - u, u))
    x = v * (2.0 * math.pi / 96.0)
    y = x * x
    r = jnp.float32(1.0 / 6227020800.0)
    for c in (-1.0 / 39916800.0, 1.0 / 362880.0, -1.0 / 5040.0, 1.0 / 120.0, -1.0 / 6.0, 1.0):
        r = r * y + c
    return x * r


def cosine(turns):
    return sine(turns + 24.0)


def cmul(a, b):
    return (a[0] * b[0] - a[1] * b[1], a[0] * b[1] + a[1] * b[0])


def cadd(a, b):
    return (a[0] + b[0], a[1] + b[1])


def csub(a, b):
    return (a[0] - b[0], a[1] - b[1])


def start_loads(s_hbm, buf, sem):
    for t in range(3):
        for c in range(4 * t, 4 * t + 4):
            pltpu.make_async_copy(
                s_hbm.at[:, :, :, :, pl.ds(128 * c, 128)], buf.at[:, :, :, c], sem.at[t]
            ).start()


def wait_load(buf, sem, t):
    part = buf.at[:, :, :, 4 * t : 4 * t + 4]
    pltpu.make_async_copy(part, part, sem.at[t]).wait()


def fill_phases(mom, rhs, tab):
    x3 = lax.broadcasted_iota(jnp.int32, (96, 128), 0).astype(jnp.float32)
    c3 = cosine(mom[2:3] * x3)
    s3 = sine(mom[2:3] * x3)
    x2 = lax.broadcasted_iota(jnp.int32, (16, 128), 0).astype(jnp.float32)
    tab[0] = cosine(mom[1:2] * x2)
    tab[1] = sine(mom[1:2] * x2)

    def row(b, _):
        c2 = tab[0, pl.ds(b, 1), :]
        s2 = tab[1, pl.ds(b, 1), :]
        at = pl.ds(pl.multiple_of(96 * b, 96), 96)
        rhs[at, 0:128] = (c2 * c3 - s2 * s3).astype(jnp.bfloat16)
        rhs[at, 128:256] = (s2 * c3 + c2 * s3).astype(jnp.bfloat16)
        return 0

    lax.fori_loop(0, 16, row, 0)


def blocks(t, y, buf, sem, wide, skp, lhs):
    low = lax.broadcasted_iota(jnp.int32, (8, 128), 0) < 4

    def rot(v):
        return pltpu.roll(v, 4, 0)

    def widen(i, _):
        for part in range(2):
            for row in range(12):
                wide[part, row, i] = (
                    buf[part, row, i, 4 * t : 4 * t + 4].reshape(16, 128).astype(jnp.float32)
                )
        return 0

    def load(part, row, i, h):
        return wide[part, row, i, 8 * h : 8 * h + 8]

    def pack_k(kp, _):
        for c in range(3):
            made = []
            for part in range(2):
                four = []
                for h in range(2):
                    ah = load(part, 4 * c, 2 * kp, h)
                    bh = load(part, 4 * c, 2 * kp + 1, h)
                    four.append(jnp.where(low, ah, rot(bh)))
                    four.append(jnp.where(low, rot(ah), bh))
                made.append(four)
            for ch in range(4):
                re, im = made[0][ch], made[1][ch]
                skp[ch, 0, c, kp] = re
                skp[ch, 1, c, kp] = im
                skp[ch, 2, c, kp] = re + im
        return 0

    def spins(idx, h):
        return [
            [(load(0, 4 * a + s, idx, h), load(1, 4 * a + s, idx, h)) for s in range(4)]
            for a in range(3)
        ]

    def pair(p, _):
        e = PAIRS * y + p
        d = e // 12
        i = e - 12 * d
        j = lax.rem(i + d, 12)
        for h in range(2):
            xh, yh = spins(i, h), spins(j, h)
            q = {}
            for a, b, c in COLOURS:
                total = None
                for s, u in ((0, 1), (2, 3)):
                    term = csub(cmul(xh[a][s], yh[b][u]), cmul(xh[a][u], yh[b][s]))
                    more = csub(cmul(yh[a][s], xh[b][u]), cmul(yh[a][u], xh[b][s]))
                    term = cadd(term, more)
                    total = term if total is None else cadd(total, term)
                re, im = total
                q[c] = (re, im)
            for odd in range(2):
                ch = 2 * h + odd
                dup = {}
                for c in range(3):
                    both = []
                    for v in q[c]:
                        r = rot(v)
                        both.append(jnp.where(low, r, v) if odd else jnp.where(low, v, r))
                    dup[c] = both + [both[0] + both[1]]
                for kq in range(3):
                    halves = []
                    for kp in (2 * kq, 2 * kq + 1):
                        tot = []
                        for part in range(3):
                            tot.append(
                                dup[0][part] * skp[ch, part, 0, kp]
                                + dup[1][part] * skp[ch, part, 1, kp]
                                + dup[2][part] * skp[ch, part, 2, kp]
                            )
                        halves.append((tot[0] - tot[1], tot[2] - tot[0] - tot[1]))
                    for part in range(2):
                        rows = pl.ds(pl.multiple_of(96 * p + 48 * part + 16 * kq, 16), 16)
                        lanes = slice(512 * t + 128 * ch, 512 * t + 128 * ch + 128)
                        lhs[rows, lanes] = jnp.concatenate(
                            [halves[0][part], halves[1][part]], axis=0
                        ).astype(jnp.bfloat16)
        return 0

    wait_load(buf, sem, t)
    lax.fori_loop(0, 12, widen, 0)
    lax.fori_loop(0, 6, pack_k, 0)
    lax.fori_loop(0, PAIRS, pair, 0)


def finish(mom, x0, y0, scale, chan, acc, zbuf, part1):
    x1 = lax.broadcasted_iota(jnp.int32, (8, 128), 0) % 4 + x0
    turns = mom[0:1] * x1.astype(jnp.float32) + mom[1:2] * y0.astype(jnp.float32)
    fc, fs = cosine(turns) * scale, sine(turns) * scale

    def pair(p, _):
        for g in range(6):
            r = acc[pl.ds(pl.multiple_of(96 * p + 8 * g, 8), 8), :]
            m = acc[pl.ds(pl.multiple_of(96 * p + 48 + 8 * g, 8), 8), :]
            re = r[:, :128] + m[:, 128:]
            im = m[:, :128] - r[:, 128:]
            at = pl.ds(pl.multiple_of(48 * p + 8 * g, 8), 8)
            zbuf[0, at, :] = fc * re + fs * im
            zbuf[1, at, :] = fc * im - fs * re
        return 0

    lax.fori_loop(0, PAIRS, pair, 0)
    zbuf[:, 480:512, :] = jnp.zeros((2, 32, 128), jnp.float32)
    for part in range(2):
        tot = zbuf[part, pl.ds(0, 128, stride=4), :]
        for k in range(1, 4):
            tot = tot + zbuf[part, pl.ds(k, 128, stride=4), :]
        turned = tot.T
        for g in range(8):
            part1[g, IM * part : IM * part + 16, :] = turned[16 * g : 16 * g + 16]
    for g in range(8):
        for k in range(4):
            n = chan[k % 2, 2 * g + k // 2]
            for part in range(2):
                row = part1[pl.ds(n // 16, 1), pl.ds(IM * part + n % 16, 1), :]
                at = 16 + 2 * k + part
                part1[g : g + 1, at : at + 1, :] = row


def place(m):
    i = jnp.floor((m + 0.5) * (1.0 / 144.0))
    r = m - 144.0 * i
    j = jnp.floor((r + 0.5) * (1.0 / 12.0))
    k = r - 12.0 * j
    d = j - i
    d = jnp.where(d < 0.0, d + 12.0, d)
    flip = (d > 6.0) | ((d == 6.0) & (i >= 6.0))
    e = jnp.where(flip, 12.0 * (12.0 - d) + j, 12.0 * d + i)
    slot = jnp.floor((e + 0.5) * (1.0 / PAIRS))
    return slot, (e - PAIRS * slot) * 12.0 + k


def pick(x, lane):
    return jnp.take_along_axis(x, lane, axis=1, mode="promise_in_bounds")


def kernel(
    s_hbm, momenta_hbm, chan_hbm, tindex_hbm, tweight_hbm, lengths_hbm, out, corr,
    buf, wide, rhs, tab, skp, lhs, acc, zbuf, momenta, chan, tindex, tweight, lengths,
    mom_box, term_box, term_all, part1, got1, sum1, got2, part3, got3, cols,
    load_sem, small_sem, send_sem, recv_sem,
):
    sx, x, y = lax.axis_index("sx"), lax.axis_index("sy"), lax.axis_index("mom")
    z, core = sx // 2, lax.rem(sx, 2)
    b = 4 * core + x

    def b_dev(g, plane):
        return (2 * z + g // 4, lax.rem(g, 4), plane)

    def z_dev(g):
        return (2 * g + core, x, y)

    def y_dev(g):
        return (sx, x, g)

    def step(v, o):
        return lax.rem(v + o, 8)

    def copy(src, dst, stage, o, dev, arrive=None):
        return pltpu.make_async_remote_copy(
            src_ref=src, dst_ref=dst, send_sem=send_sem.at[stage, o],
            recv_sem=recv_sem.at[stage, o if arrive is None else arrive], device_id=dev,
            device_id_type=pl.DeviceIdType.MESH,
        )

    smalls = [
        pltpu.make_async_copy(src, dst, small_sem.at[k])
        for k, (src, dst) in enumerate(
            (
                (momenta_hbm, momenta), (tindex_hbm, tindex), (tweight_hbm, tweight),
                (lengths_hbm, lengths), (chan_hbm, chan),
            )
        )
    ]
    for c in smalls:
        c.start()
    start_loads(s_hbm, buf, load_sem)
    barrier = pltpu.get_barrier_semaphore()

    def greet(dev):
        pl.semaphore_signal(barrier, inc=1, device_id=dev, device_id_type=pl.DeviceIdType.MESH)

    alone = b == y
    for o in range(1, 8):
        greet(b_dev(step(b, o), y))
        greet(z_dev(step(z, o)))
        greet(y_dev(step(y, o)))
        greet(b_dev(y, step(y, o)))

    @pl.when(jnp.logical_not(alone))
    def _():
        greet(b_dev(y, y))

    rows = lax.broadcasted_iota(jnp.int32, (8, 128), 0)
    lanes = lax.broadcasted_iota(jnp.int32, (8, 128), 1)
    for c in smalls:
        c.wait()
    mom_box[0] = jnp.zeros((8, 128), jnp.float32)
    mom_box[0, 0:3, 0:16] = momenta[...].astype(jnp.float32)
    mom_box[0] = pltpu.roll(mom_box[0], 16 * y, 1)
    term_box[0] = jnp.zeros((8, 128), jnp.float32)
    live = lax.broadcasted_iota(jnp.int32, (2, 24), 1) + (8 * z + b) * 24
    owner = lax.broadcasted_iota(jnp.int32, (2, 24), 0)
    size = jnp.where(owner == 0, lengths[0], lengths[1])
    for side in range(2):
        slot, lane = place(tindex[side].astype(jnp.float32))
        term_box[0, 2 * side : 2 * side + 2, 0:24] = slot * 128.0 + lane
    term_box[0, 4:6, 0:24] = jnp.where(live < size, tweight[...], 0.0)
    term_box[0] = pltpu.roll(term_box[0], 32 * lax.rem(b, 4), 1)
    slot, lane = place((lanes + 54 * (8 * lax.rem(z, 4) + rows)).astype(jnp.float32))
    cols[0] = slot
    cols[1] = lane

    blocks(0, y, buf, load_sem, wide, skp, lhs)

    pl.semaphore_wait(barrier, jnp.where(alone, 28, 29))
    sent = []
    for o in range(1, 8):
        c = copy(mom_box.at[0], mom_box.at[o], 0, o, y_dev(step(y, o)))
        c.start()
        sent.append(c)
    boxes = []
    for o in range(1, 8):
        c = copy(term_box.at[0], term_box.at[o], 1, o, b_dev(step(b, o), y))
        c.start()
        boxes.append(c)

    blocks(1, y, buf, load_sem, wide, skp, lhs)

    for c in boxes:
        c.wait_recv()
    for half in range(2):
        joined = jnp.zeros((8, 128), jnp.float32)
        for o in range(8):
            source = lax.rem(b + 8 - o, 8)
            joined = joined + jnp.where(source // 4 == half, term_box[o], 0.0)
        term_all[z, half] = joined
    sent += boxes
    boxes = []
    for o in range(1, 8):
        c = copy(term_all.at[z], term_all.at[z], 2, o, z_dev(step(z, o)))
        c.start()
        boxes.append(c)

    blocks(2, y, buf, load_sem, wide, skp, lhs)
    for c in sent[:7]:
        c.wait_recv()
    mom = mom_box[0]
    for o in range(1, 8):
        mom = mom + mom_box[o]
    fill_phases(mom, rhs, tab)
    acc[...] = jnp.dot(lhs[...], rhs[...], preferred_element_type=jnp.float32)
    finish(mom, 4 * sx, 16 * x, SCALE, chan, acc, zbuf, part1)

    hops = []
    for o in range(1, 8):
        g = step(b, o)
        c = copy(part1.at[g], got1.at[o], 3, o, b_dev(g, y))
        c.start()
        hops.append(c)
    total = part1[b]
    for c in hops:
        c.wait_recv()
    for o in range(1, 8):
        total = total + got1[o]
    sum1[...] = total
    sent += hops

    hops = []
    for o in range(1, 8):
        g = step(z, o)
        c = copy(
            sum1.at[pl.ds(pl.multiple_of(16 * (g // 4), 8), 24)], got2.at[o], 4, o, z_dev(g)
        )
        c.start()
        hops.append(c)
    low = z < 4
    total = jnp.where(low, sum1[0:24], sum1[16:40])
    for c in boxes:
        c.wait_recv()
    sent += boxes
    for c in hops:
        c.wait_recv()
    for o in range(1, 8):
        total = total + got2[o]
    sent += hops
    table = jnp.where(low, total[0:16], total[8:24])
    rest = jnp.where(low, total[16:24], total[0:8])
    for g in range(8):
        lane = jnp.broadcast_to(cols[1, g : g + 1], (8, 128)).astype(jnp.int32)
        mine = jnp.broadcast_to(cols[0, g : g + 1], (8, 128)) == y.astype(jnp.float32)
        for u in range(2):
            part3[g, 8 * u : 8 * u + 8] = jnp.where(mine, pick(table[8 * u : 8 * u + 8], lane), 0.0)
        part3[g, 16:24] = rest

    def third(o, arrive):
        g = step(b, o)
        return copy(part3.at[g], got3.at[arrive], 5, o, b_dev(g, b), arrive)

    for o in range(1, 8):
        third(o, y).start()

    @pl.when(jnp.logical_not(alone))
    def _():
        third(0, y).start()

    @pl.when(alone)
    def _():
        got3[y] = part3[y]

    terms = [term_all[:, :, k, :].reshape(16, 128) for k in range(6)]
    places = []
    for k in range(4):
        slot = jnp.floor((terms[k] + 0.5) * (1.0 / 128.0))
        places.append((slot, (terms[k] - 128.0 * slot).astype(jnp.int32)))

    for k in range(8):
        @pl.when(jnp.logical_not(alone & (y == k)))
        def _():
            third(0, k).wait_recv()

    whole = got3[0, 0:16]
    for k in range(1, 8):
        whole = whole + got3[k, 0:16]
    out[...] = whole[:, :54]

    answer = jnp.zeros((2, 2), jnp.float32)
    at_row = lax.broadcasted_iota(jnp.int32, (2, 2), 0)
    at_col = lax.broadcasted_iota(jnp.int32, (2, 2), 1)
    for h in range(2):
        sides = []
        for side in range(2):
            slot, lane = places[2 * side + h]
            both = []
            for part in range(2):
                row = 16 + 4 * h + 2 * side + part
                chosen = []
                for u in range(2):
                    value = jnp.zeros((8, 128), jnp.float32)
                    for k in range(8):
                        have = jnp.broadcast_to(got3[k, row : row + 1], (8, 128))
                        have = pick(have, lane[8 * u : 8 * u + 8])
                        value = jnp.where(slot[8 * u : 8 * u + 8] == k, have, value)
                    chosen.append(value)
                both.append(jnp.concatenate(chosen, axis=0))
            sides.append(tuple(both))
        prod = cmul(sides[0], sides[1])
        for part in range(2):
            answer = jnp.where(
                (at_row == part) & (at_col == h), jnp.sum(terms[4 + h] * prod[part]), answer
            )
    corr[...] = answer

    for c in sent:
        c.wait_send()
    for o in range(1, 8):
        third(o, y).wait_send()

    @pl.when(jnp.logical_not(alone))
    def _():
        third(0, y).wait_send()


def local(propagator, momenta, chan_moms, term_index, term_weight, lengths):
    f32, i32 = jnp.float32, jnp.int32
    vmem = pl.BlockSpec(memory_space=pltpu.VMEM)
    return pl.pallas_call(
        kernel,
        out_shape=(
            jax.ShapeDtypeStruct((16, 54), f32),
            jax.ShapeDtypeStruct((2, 2), f32),
        ),
        in_specs=[pl.BlockSpec(memory_space=pl.ANY)] * 6,
        out_specs=(vmem, vmem),
        scratch_shapes=[
            pltpu.VMEM((2, 12, 12, 12, 4, 128), jnp.bfloat16),
            pltpu.VMEM((2, 12, 12, 16, 128), f32),
            pltpu.VMEM((1536, 256), jnp.bfloat16),
            pltpu.VMEM((2, 16, 128), f32),
            pltpu.VMEM((4, 3, 3, 6, 8, 128), f32),
            pltpu.VMEM((96 * PAIRS, 1536), jnp.bfloat16),
            pltpu.VMEM((96 * PAIRS, 256), f32),
            pltpu.VMEM((2, 512, 128), f32),
            pltpu.VMEM((3, 16), i32),
            pltpu.SMEM((2, 16), i32),
            pltpu.VMEM((2, 2, 24), i32),
            pltpu.VMEM((2, 24), f32),
            pltpu.SMEM((2,), i32),
            pltpu.VMEM((8, 8, 128), f32),
            pltpu.VMEM((8, 8, 128), f32),
            pltpu.VMEM((8, 2, 8, 128), f32),
            pltpu.VMEM((8, 40, 128), f32),
            pltpu.VMEM((8, 40, 128), f32),
            pltpu.VMEM((40, 128), f32),
            pltpu.VMEM((8, 24, 128), f32),
            pltpu.VMEM((8, 24, 128), f32),
            pltpu.VMEM((8, 24, 128), f32),
            pltpu.VMEM((2, 8, 128), f32),
            pltpu.SemaphoreType.DMA((3,)),
            pltpu.SemaphoreType.DMA((5,)),
            pltpu.SemaphoreType.DMA((6, 8)),
            pltpu.SemaphoreType.DMA((6, 8)),
        ],
        compiler_params=pltpu.CompilerParams(
            collective_id=0, has_side_effects=True, vmem_limit_bytes=62 * 2**20
        ),
    )(propagator, momenta.T, chan_moms.T, term_index, term_weight, lengths)


def solution(mesh):
    in_specs = (
        P(None, None, None, "sx", "sy"),
        P("mom", None),
        P(),
        P(None, "mom", ("sx", "sy")),
        P("mom", ("sx", "sy")),
        P("mom"),
    )
    out_specs = (P("mom", ("sx", "sy")), P(None, "mom"))
    return jax.shard_map(local, mesh=mesh, in_specs=in_specs, out_specs=out_specs, check_vma=False)
```

time: 53.4 us -> 44 us (0.82)
  Pallas kernels: 45.8 us -> 40.7 us
  local copies, waits for them, and re-layouts: 6.69 us -> 2.51 us
    pallas_call x1, Pallas kernels: 45.8 us -> 40.7 us  [local(): pl.pallas_call(kernel, out_shape=(jax.ShapeDtypeStruct((16, 54), f32), ja...]
    unnamed x12 -> x2, local copies, waits for them, and re-layouts: 6.69 us -> 2.51 us
where the time goes in v2:
time: 44 us; the launch traced here: 43.8 us
  Pallas kernels  40.7 us (93%)
  local copies, waits for them, and re-layouts  2.51 us (6%)
  between operations  0.64 us (1%)
    pallas_call x1, Pallas kernels, local(): pl.pallas_call(kernel, out_shape=(jax.ShapeDtypeStruct((16, 54), f32), ja...  40.7 us
    unnamed x2, local copies, waits for them, and re-layouts  2.51 us

profile of v2, /device:TPU:1, one launch (start us, length us, event | category | flops | bytes accessed | tf_op | source)
XLA Modules:
  0.0 43.8 jit_solution(7287342287674180577)
XLA Ops:
  0.6 40.7 %shard_map.77 = (f32[16,54]{1,0:T(8,128)}, f32[2,2]{1,0:T(2,128)}) custom-call(bf16[2,12,12,4,1536]{4,3,2,1,0:T(4,128)(2,1)} %s_hbm.1, s32[3,16]{1,0:T(4,128)} %bitcast.2, s32[2,16]{1,0:T(2,128)} %bitcast.3, s32[2,2,24]{2,1,0:T(2,128)} %tindex_hbm.1, f32[2,24]{1,0:T(2,128)} %tweight_hbm.1, s32[2]{0:T(128)} %lengths_hbm.1), custom_call_target="tpu_custom_call" | custom-call | tf_op jit(solution)/shard_map/pallas_call | solution.py:448
  41.3 1.3 %copy.10 = f32[16,54]{1,0:T(8,128)} copy(f32[16,54]{1,0:T(8,128)} %get-tuple-element.4) | data formatting | bytes 6912
  42.6 1.2 %copy.11 = f32[2,2]{1,0:T(2,128)} copy(f32[2,2]{1,0:T(2,128)} %get-tuple-element.5) | data formatting | bytes 32

commit v3 on v2

--- a/solution.py
+++ b/solution.py
@@ -53,13 +53,17 @@
     pltpu.make_async_copy(part, part, sem.at[t]).wait()
 
 
-def fill_phases(mom, rhs, tab):
+def fill_phases(rhs, tab):
+    lane = lax.broadcasted_iota(jnp.int32, (1, 128), 1).astype(jnp.float32)
+    p2 = jnp.floor((lane + 0.5) * (1.0 / 9.0))
+    p3 = lane - 9.0 * p2 - 4.0
+    p2 = p2 - 4.0
     x3 = lax.broadcasted_iota(jnp.int32, (96, 128), 0).astype(jnp.float32)
-    c3 = cosine(mom[2:3] * x3)
-    s3 = sine(mom[2:3] * x3)
+    c3 = cosine(p3 * x3)
+    s3 = sine(p3 * x3)
     x2 = lax.broadcasted_iota(jnp.int32, (16, 128), 0).astype(jnp.float32)
-    tab[0] = cosine(mom[1:2] * x2)
-    tab[1] = sine(mom[1:2] * x2)
+    tab[0] = cosine(p2 * x2)
+    tab[1] = sine(p2 * x2)
 
     def row(b, _):
         c2 = tab[0, pl.ds(b, 1), :]
@@ -161,20 +165,26 @@
     wait_load(buf, sem, t)
     lax.fori_loop(0, 12, widen, 0)
     lax.fori_loop(0, 6, pack_k, 0)
-    lax.fori_loop(0, PAIRS, pair, 0)
+    lax.fori_loop(0, PAIRS, pair, 0, unroll=2)
+
+
+def pick(x, lane):
+    return jnp.take_along_axis(x, lane, axis=1, mode="promise_in_bounds")
 
 
 def finish(mom, x0, y0, scale, chan, acc, zbuf, part1):
     x1 = lax.broadcasted_iota(jnp.int32, (8, 128), 0) % 4 + x0
     turns = mom[0:1] * x1.astype(jnp.float32) + mom[1:2] * y0.astype(jnp.float32)
     fc, fs = cosine(turns) * scale, sine(turns) * scale
+    cell = (9.0 * mom[1:2] + mom[2:3] + 40.0).astype(jnp.int32)
+    cell = jnp.broadcast_to(cell, (8, 128))
 
     def pair(p, _):
         for g in range(6):
             r = acc[pl.ds(pl.multiple_of(96 * p + 8 * g, 8), 8), :]
             m = acc[pl.ds(pl.multiple_of(96 * p + 48 + 8 * g, 8), 8), :]
-            re = r[:, :128] + m[:, 128:]
-            im = m[:, :128] - r[:, 128:]
+            re = pick(r[:, :128] + m[:, 128:], cell)
+            im = pick(m[:, :128] - r[:, 128:], cell)
             at = pl.ds(pl.multiple_of(48 * p + 8 * g, 8), 8)
             zbuf[0, at, :] = fc * re + fs * im
             zbuf[1, at, :] = fc * im - fs * re
@@ -198,7 +208,7 @@
                 part1[g : g + 1, at : at + 1, :] = row
 
 
-def place(m):
+def locate(m):
     i = jnp.floor((m + 0.5) * (1.0 / 144.0))
     r = m - 144.0 * i
     j = jnp.floor((r + 0.5) * (1.0 / 12.0))
@@ -208,11 +218,14 @@
     flip = (d > 6.0) | ((d == 6.0) & (i >= 6.0))
     e = jnp.where(flip, 12.0 * (12.0 - d) + j, 12.0 * d + i)
     slot = jnp.floor((e + 0.5) * (1.0 / PAIRS))
-    return slot, (e - PAIRS * slot) * 12.0 + k
-
-
-def pick(x, lane):
-    return jnp.take_along_axis(x, lane, axis=1, mode="promise_in_bounds")
+    odd = i - 2.0 * jnp.floor(0.5 * i)
+    kind = jnp.where(flip, 1.0 - odd, odd)
+    return slot, e - PAIRS * slot, k, kind
+
+
+def place(m):
+    slot, inner, k, _ = locate(m)
+    return slot, inner * 12.0 + k
 
 
 def kernel(
@@ -272,6 +285,7 @@
     def _():
         greet(b_dev(y, y))
 
+    fill_phases(rhs, tab)
     rows = lax.broadcasted_iota(jnp.int32, (8, 128), 0)
     lanes = lax.broadcasted_iota(jnp.int32, (8, 128), 1)
     for c in smalls:
@@ -288,9 +302,18 @@
         term_box[0, 2 * side : 2 * side + 2, 0:24] = slot * 128.0 + lane
     term_box[0, 4:6, 0:24] = jnp.where(live < size, tweight[...], 0.0)
     term_box[0] = pltpu.roll(term_box[0], 32 * lax.rem(b, 4), 1)
-    slot, lane = place((lanes + 54 * (8 * lax.rem(z, 4) + rows)).astype(jnp.float32))
-    cols[0] = slot
-    cols[1] = lane
+    slot, inner, k, kind = locate((lanes + 54 * (8 * lax.rem(z, 4) + rows)).astype(jnp.float32))
+    mine = (slot == y.astype(jnp.float32)) & (lanes < 54)
+    held = [
+        jnp.max(jnp.where(mine & (kind == v), inner, 0.0), axis=1, keepdims=True) for v in range(2)
+    ]
+    within = lax.rem(lanes, 32)
+    second = within >= 12
+    cols[0] = jnp.where(second, held[1], held[0]) * 12.0 + jnp.where(
+        second, within - 12, within
+    ).astype(jnp.float32)
+    cols[1] = slot
+    cols[2] = 12.0 * kind + k
 
     blocks(0, y, buf, load_sem, wide, skp, lhs)
 
@@ -308,6 +331,21 @@
 
     blocks(1, y, buf, load_sem, wide, skp, lhs)
 
+    blocks(2, y, buf, load_sem, wide, skp, lhs)
+    acc[...] = jnp.dot(lhs[...], rhs[...], preferred_element_type=jnp.float32)
+    for c in sent[:7]:
+        c.wait_recv()
+    mom = mom_box[0]
+    for o in range(1, 8):
+        mom = mom + mom_box[o]
+    finish(mom, 4 * sx, 16 * x, SCALE, chan, acc, zbuf, part1)
+
+    hops = []
+    for o in range(1, 8):
+        g = step(b, o)
+        c = copy(part1.at[g], got1.at[o], 3, o, b_dev(g, y))
+        c.start()
+        hops.append(c)
     for c in boxes:
         c.wait_recv()
     for half in range(2):
@@ -322,23 +360,6 @@
         c = copy(term_all.at[z], term_all.at[z], 2, o, z_dev(step(z, o)))
         c.start()
         boxes.append(c)
-
-    blocks(2, y, buf, load_sem, wide, skp, lhs)
-    for c in sent[:7]:
-        c.wait_recv()
-    mom = mom_box[0]
-    for o in range(1, 8):
-        mom = mom + mom_box[o]
-    fill_phases(mom, rhs, tab)
-    acc[...] = jnp.dot(lhs[...], rhs[...], preferred_element_type=jnp.float32)
-    finish(mom, 4 * sx, 16 * x, SCALE, chan, acc, zbuf, part1)
-
-    hops = []
-    for o in range(1, 8):
-        g = step(b, o)
-        c = copy(part1.at[g], got1.at[o], 3, o, b_dev(g, y))
-        c.start()
-        hops.append(c)
     total = part1[b]
     for c in hops:
         c.wait_recv()
@@ -357,9 +378,6 @@
         hops.append(c)
     low = z < 4
     total = jnp.where(low, sum1[0:24], sum1[16:40])
-    for c in boxes:
-        c.wait_recv()
-    sent += boxes
     for c in hops:
         c.wait_recv()
     for o in range(1, 8):
@@ -368,11 +386,13 @@
     table = jnp.where(low, total[0:16], total[8:24])
     rest = jnp.where(low, total[16:24], total[0:8])
     for g in range(8):
-        lane = jnp.broadcast_to(cols[1, g : g + 1], (8, 128)).astype(jnp.int32)
-        mine = jnp.broadcast_to(cols[0, g : g + 1], (8, 128)) == y.astype(jnp.float32)
+        lane = jnp.broadcast_to(cols[0, g : g + 1], (8, 128)).astype(jnp.int32)
+        packed = []
         for u in range(2):
-            part3[g, 8 * u : 8 * u + 8] = jnp.where(mine, pick(table[8 * u : 8 * u + 8], lane), 0.0)
-        part3[g, 16:24] = rest
+            have = pick(table[8 * u : 8 * u + 8], lane)
+            packed.append(jnp.where(lax.rem(lanes // 32, 2) == 1, pltpu.roll(have, 4, 0), have))
+        part3[g, 0:8] = rest
+        part3[g, 8:12] = jnp.where(lanes < 64, packed[0], packed[1])[0:4]
 
     def third(o, arrive):
         g = step(b, o)
@@ -389,6 +409,9 @@
     def _():
         got3[y] = part3[y]
 
+    for c in boxes:
+        c.wait_recv()
+    sent += boxes
     terms = [term_all[:, :, k, :].reshape(16, 128) for k in range(6)]
     places = []
     for k in range(4):
@@ -400,10 +423,17 @@
         def _():
             third(0, k).wait_recv()
 
-    whole = got3[0, 0:16]
-    for k in range(1, 8):
-        whole = whole + got3[k, 0:16]
-    out[...] = whole[:, :54]
+    slot = jnp.broadcast_to(cols[1, pl.ds(b, 1), :], (8, 128))
+    lane = jnp.broadcast_to(cols[2, pl.ds(b, 1), :], (8, 128)).astype(jnp.int32)
+    quads = [jnp.zeros((8, 128), jnp.float32) for g in range(4)]
+    for v in range(4):
+        have = jnp.concatenate([got3[2 * v, 8:12], got3[2 * v + 1, 8:12]], axis=0)
+        here = slot == jnp.where(rows < 4, 2.0 * v, 2.0 * v + 1.0)
+        for g in range(4):
+            quads[g] = jnp.where(here, pick(have, lane + 32 * g), quads[g])
+    for g in range(4):
+        whole = quads[g] + pltpu.roll(quads[g], 4, 0)
+        out[4 * g : 4 * g + 4, :] = whole[0:4, :54]
 
     answer = jnp.zeros((2, 2), jnp.float32)
     at_row = lax.broadcasted_iota(jnp.int32, (2, 2), 0)
@@ -414,7 +444,7 @@
             slot, lane = places[2 * side + h]
             both = []
             for part in range(2):
-                row = 16 + 4 * h + 2 * side + part
+                row = 4 * h + 2 * side + part
                 chosen = []
                 for u in range(2):
                     value = jnp.zeros((8, 128), jnp.float32)
@@ -442,14 +472,25 @@
         third(0, y).wait_send()
 
 
+def hand_over(block, value, out, corr, sem):
+    copies = [
+        pltpu.make_async_copy(block, out, sem.at[0]),
+        pltpu.make_async_copy(value, corr, sem.at[1]),
+    ]
+    for c in copies:
+        c.start()
+    for c in copies:
+        c.wait()
+
+
 def local(propagator, momenta, chan_moms, term_index, term_weight, lengths):
     f32, i32 = jnp.float32, jnp.int32
     vmem = pl.BlockSpec(memory_space=pltpu.VMEM)
-    return pl.pallas_call(
+    results = pl.pallas_call(
         kernel,
         out_shape=(
-            jax.ShapeDtypeStruct((16, 54), f32),
-            jax.ShapeDtypeStruct((2, 2), f32),
+            pltpu.VMEM((16, 54), f32),
+            pltpu.VMEM((2, 2), f32),
         ),
         in_specs=[pl.BlockSpec(memory_space=pl.ANY)] * 6,
         out_specs=(vmem, vmem),
@@ -474,9 +515,9 @@
             pltpu.VMEM((8, 40, 128), f32),
             pltpu.VMEM((40, 128), f32),
             pltpu.VMEM((8, 24, 128), f32),
-            pltpu.VMEM((8, 24, 128), f32),
-            pltpu.VMEM((8, 24, 128), f32),
-            pltpu.VMEM((2, 8, 128), f32),
+            pltpu.VMEM((8, 12, 128), f32),
+            pltpu.VMEM((8, 12, 128), f32),
+            pltpu.VMEM((3, 8, 128), f32),
             pltpu.SemaphoreType.DMA((3,)),
             pltpu.SemaphoreType.DMA((5,)),
             pltpu.SemaphoreType.DMA((6, 8)),
@@ -486,6 +527,17 @@
             collective_id=0, has_side_effects=True, vmem_limit_bytes=62 * 2**20
         ),
     )(propagator, momenta.T, chan_moms.T, term_index, term_weight, lengths)
+    return pl.pallas_call(
+        hand_over,
+        out_shape=(
+            jax.ShapeDtypeStruct((16, 54), f32),
+            jax.ShapeDtypeStruct((2, 2), f32),
+        ),
+        in_specs=[vmem] * 2,
+        out_specs=[pl.BlockSpec(memory_space=pl.ANY)] * 2,
+        scratch_shapes=[pltpu.SemaphoreType.DMA((2,))],
+        compiler_params=pltpu.CompilerParams(vmem_limit_bytes=2**20),
+    )(*results)
 
 
 def solution(mesh):

time: 44 us -> 38.4 us (0.87)
  Pallas kernels: 40.7 us -> 37.7 us
  local copies, waits for them, and re-layouts: 2.51 us -> 0 us
    pallas_call x1 -> x2, Pallas kernels: 40.7 us -> 37.7 us  [the longest x1 37 us: local(): pl.pallas_call(kernel, out_shape=(pltpu.VMEM((16, 54), f32), pltpu.VMEM((...]
    unnamed x2 -> x0, local copies, waits for them, and re-layouts: 2.51 us -> none
where the time goes in v3:
time: 38.4 us; the launch traced here: 38.3 us
  Pallas kernels  37.7 us (98%)
  between operations  0.64 us (2%)
    pallas_call x1, Pallas kernels, local(): pl.pallas_call(kernel, out_shape=(pltpu.VMEM((16, 54), f32), pltpu.VMEM((...  37 us

profile of v3, /device:TPU:1, one launch (start us, length us, event | category | flops | bytes accessed | tf_op | source)
XLA Modules:
  0.0 38.3 jit_solution(1853476090426425785)
XLA Ops:
  0.6 37.0 %shard_map.77 = (f32[16,54]{1,0:T(8,128)S(1)}, f32[2,2]{1,0:T(2,128)S(1)}) custom-call(bf16[2,12,12,4,1536]{4,3,2,1,0:T(4,128)(2,1)} %s_hbm.1, s32[3,16]{1,0:T(4,128)} %bitcast.2, s32[2,16]{1,0:T(2,128)} %bitcast.3, s32[2,2,24]{2,1,0:T(2,128)} %tindex_hbm.1, f32[2,24]{1,0:T(2,128)} %tweight_hbm.1, s32[2]{0:T(128)} %lengths_hbm.1), custom_call_target="tpu_custom_call" | custom-call | tf_op jit(solution)/shard_map/pallas_call | solution.py:489
  37.7 0.6 %shard_map.78 = (f32[16,54]{1,0:T(8,128)}, f32[2,2]{1,0:T(2,128)}) custom-call(f32[16,54]{1,0:T(8,128)S(1)} %get-tuple-element.4.block, f32[2,2]{1,0:T(2,128)S(1)} %get-tuple-element.5.value), custom_call_target="tpu_custom_call" | custom-call | tf_op jit(solution)/shard_map/pallas_call | solution.py:530

commit v4 on v3

--- a/solution.py
+++ b/solution.py
@@ -10,6 +10,7 @@
 PAIRS = 10
 SCALE = 1.0 / math.sqrt(393216)
 IM = 24
+FAR = (4, 3, 5, 2, 6, 1, 7)
 COLOURS = ((1, 2, 0), (2, 0, 1), (0, 1, 2))
 
 
@@ -40,8 +41,8 @@
     return (a[0] - b[0], a[1] - b[1])
 
 
-def start_loads(s_hbm, buf, sem):
-    for t in range(3):
+def start_loads(s_hbm, buf, sem, thirds):
+    for t in thirds:
         for c in range(4 * t, 4 * t + 4):
             pltpu.make_async_copy(
                 s_hbm.at[:, :, :, :, pl.ds(128 * c, 128)], buf.at[:, :, :, c], sem.at[t]
@@ -49,7 +50,7 @@
 
 
 def wait_load(buf, sem, t):
-    part = buf.at[:, :, :, 4 * t : 4 * t + 4]
+    part = buf.at[:, :, :, pl.ds(4 * t, 4)]
     pltpu.make_async_copy(part, part, sem.at[t]).wait()
 
 
@@ -76,7 +77,7 @@
     lax.fori_loop(0, 16, row, 0)
 
 
-def blocks(t, y, buf, sem, wide, skp, lhs):
+def blocks(t, y, buf, sem, wide, skp, lhs, rhs, acc):
     low = lax.broadcasted_iota(jnp.int32, (8, 128), 0) < 4
 
     def rot(v):
@@ -86,7 +87,7 @@
         for part in range(2):
             for row in range(12):
                 wide[part, row, i] = (
-                    buf[part, row, i, 4 * t : 4 * t + 4].reshape(16, 128).astype(jnp.float32)
+                    buf[part, row, i, pl.ds(4 * t, 4)].reshape(16, 128).astype(jnp.float32)
                 )
         return 0
 
@@ -156,7 +157,7 @@
                         halves.append((tot[0] - tot[1], tot[2] - tot[0] - tot[1]))
                     for part in range(2):
                         rows = pl.ds(pl.multiple_of(96 * p + 48 * part + 16 * kq, 16), 16)
-                        lanes = slice(512 * t + 128 * ch, 512 * t + 128 * ch + 128)
+                        lanes = pl.ds(pl.multiple_of(512 * t + 128 * ch, 128), 128)
                         lhs[rows, lanes] = jnp.concatenate(
                             [halves[0][part], halves[1][part]], axis=0
                         ).astype(jnp.bfloat16)
@@ -165,14 +166,24 @@
     wait_load(buf, sem, t)
     lax.fori_loop(0, 12, widen, 0)
     lax.fori_loop(0, 6, pack_k, 0)
-    lax.fori_loop(0, PAIRS, pair, 0, unroll=2)
+    def two(p, _):
+        if t:
+            rows = pl.ds(pl.multiple_of(192 * p, 64), 192)
+            depth = slice(512 * t - 512, 512 * t)
+            prod = jnp.dot(lhs[rows, depth], rhs[depth, :], preferred_element_type=jnp.float32)
+            acc[rows, :] = prod if t == 1 else acc[rows, :] + prod
+        pair(2 * p, 0)
+        pair(2 * p + 1, 0)
+        return 0
+
+    lax.fori_loop(0, PAIRS // 2, two, 0)
 
 
 def pick(x, lane):
     return jnp.take_along_axis(x, lane, axis=1, mode="promise_in_bounds")
 
 
-def finish(mom, x0, y0, scale, chan, acc, zbuf, part1):
+def finish(mom, x0, y0, scale, spots, acc, zbuf, part1):
     x1 = lax.broadcasted_iota(jnp.int32, (8, 128), 0) % 4 + x0
     turns = mom[0:1] * x1.astype(jnp.float32) + mom[1:2] * y0.astype(jnp.float32)
     fc, fs = cosine(turns) * scale, sine(turns) * scale
@@ -198,14 +209,13 @@
             tot = tot + zbuf[part, pl.ds(k, 128, stride=4), :]
         turned = tot.T
         for g in range(8):
-            part1[g, IM * part : IM * part + 16, :] = turned[16 * g : 16 * g + 16]
+            part1[40 * g + IM * part : 40 * g + IM * part + 16, :] = turned[16 * g : 16 * g + 16]
     for g in range(8):
         for k in range(4):
-            n = chan[k % 2, 2 * g + k // 2]
+            row = spots[4 * g + k]
             for part in range(2):
-                row = part1[pl.ds(n // 16, 1), pl.ds(IM * part + n % 16, 1), :]
-                at = 16 + 2 * k + part
-                part1[g : g + 1, at : at + 1, :] = row
+                at = 40 * g + 16 + 2 * k + part
+                part1[at : at + 1, :] = part1[pl.ds(row + IM * part, 1), :]
 
 
 def locate(m):
@@ -230,7 +240,7 @@
 
 def kernel(
     s_hbm, momenta_hbm, chan_hbm, tindex_hbm, tweight_hbm, lengths_hbm, out, corr,
-    buf, wide, rhs, tab, skp, lhs, acc, zbuf, momenta, chan, tindex, tweight, lengths,
+    buf, wide, rhs, tab, skp, lhs, acc, zbuf, momenta, chan, spots, tindex, tweight, lengths,
     mom_box, term_box, term_all, part1, got1, sum1, got2, part3, got3, cols,
     load_sem, small_sem, send_sem, recv_sem,
 ):
@@ -268,28 +278,35 @@
     ]
     for c in smalls:
         c.start()
-    start_loads(s_hbm, buf, load_sem)
+    start_loads(s_hbm, buf, load_sem, (0,))
     barrier = pltpu.get_barrier_semaphore()
 
     def greet(dev):
         pl.semaphore_signal(barrier, inc=1, device_id=dev, device_id_type=pl.DeviceIdType.MESH)
 
     alone = b == y
+    for o in FAR:
+        greet(y_dev(step(y, o)))
+    for o in FAR:
+        greet(z_dev(step(z, o)))
     for o in range(1, 8):
         greet(b_dev(step(b, o), y))
-        greet(z_dev(step(z, o)))
-        greet(y_dev(step(y, o)))
         greet(b_dev(y, step(y, o)))
 
     @pl.when(jnp.logical_not(alone))
     def _():
         greet(b_dev(y, y))
 
+    start_loads(s_hbm, buf, load_sem, (1, 2))
     fill_phases(rhs, tab)
     rows = lax.broadcasted_iota(jnp.int32, (8, 128), 0)
     lanes = lax.broadcasted_iota(jnp.int32, (8, 128), 1)
     for c in smalls:
         c.wait()
+    for g in range(8):
+        for k in range(4):
+            n = chan[k % 2, 2 * g + k // 2]
+            spots[4 * g + k] = 40 * (n // 16) + n % 16
     mom_box[0] = jnp.zeros((8, 128), jnp.float32)
     mom_box[0, 0:3, 0:16] = momenta[...].astype(jnp.float32)
     mom_box[0] = pltpu.roll(mom_box[0], 16 * y, 1)
@@ -302,6 +319,53 @@
         term_box[0, 2 * side : 2 * side + 2, 0:24] = slot * 128.0 + lane
     term_box[0, 4:6, 0:24] = jnp.where(live < size, tweight[...], 0.0)
     term_box[0] = pltpu.roll(term_box[0], 32 * lax.rem(b, 4), 1)
+    blocks(0, y, buf, load_sem, wide, skp, lhs, rhs, acc)
+
+    pl.semaphore_wait(barrier, jnp.where(alone, 28, 29))
+    sent = []
+    for o in range(1, 8):
+        c = copy(mom_box.at[0], mom_box.at[o], 0, o, y_dev(step(y, o)))
+        c.start()
+        sent.append(c)
+    boxes = []
+    for o in range(1, 8):
+        c = copy(term_box.at[0], term_box.at[o], 1, o, b_dev(step(b, o), y))
+        c.start()
+        boxes.append(c)
+
+
+    blocks(1, y, buf, load_sem, wide, skp, lhs, rhs, acc)
+    blocks(2, y, buf, load_sem, wide, skp, lhs, rhs, acc)
+    acc[...] += jnp.dot(lhs[:, 1024:], rhs[1024:, :], preferred_element_type=jnp.float32)
+    for c in sent[:7]:
+        c.wait_recv()
+    mom = mom_box[0]
+    for o in range(1, 8):
+        mom = mom + mom_box[o]
+    finish(mom, 4 * sx, 16 * x, SCALE, spots, acc, zbuf, part1)
+
+    hops = []
+    for o in range(1, 8):
+        g = step(b, o)
+        c = copy(
+            part1.at[pl.ds(pl.multiple_of(40 * g, 8), 40)], got1.at[o], 3, o, b_dev(g, y)
+        )
+        c.start()
+        hops.append(c)
+    for c in boxes:
+        c.wait_recv()
+    for half in range(2):
+        joined = jnp.zeros((8, 128), jnp.float32)
+        for o in range(8):
+            source = lax.rem(b + 8 - o, 8)
+            joined = joined + jnp.where(source // 4 == half, term_box[o], 0.0)
+        term_all[z, half] = joined
+    sent += boxes
+    boxes = []
+    for o in range(1, 8):
+        c = copy(term_all.at[z], term_all.at[z], 2, o, z_dev(step(z, o)))
+        c.start()
+        boxes.append(c)
     slot, inner, k, kind = locate((lanes + 54 * (8 * lax.rem(z, 4) + rows)).astype(jnp.float32))
     mine = (slot == y.astype(jnp.float32)) & (lanes < 54)
     held = [
@@ -314,53 +378,7 @@
     ).astype(jnp.float32)
     cols[1] = slot
     cols[2] = 12.0 * kind + k
-
-    blocks(0, y, buf, load_sem, wide, skp, lhs)
-
-    pl.semaphore_wait(barrier, jnp.where(alone, 28, 29))
-    sent = []
-    for o in range(1, 8):
-        c = copy(mom_box.at[0], mom_box.at[o], 0, o, y_dev(step(y, o)))
-        c.start()
-        sent.append(c)
-    boxes = []
-    for o in range(1, 8):
-        c = copy(term_box.at[0], term_box.at[o], 1, o, b_dev(step(b, o), y))
-        c.start()
-        boxes.append(c)
-
-    blocks(1, y, buf, load_sem, wide, skp, lhs)
-
-    blocks(2, y, buf, load_sem, wide, skp, lhs)
-    acc[...] = jnp.dot(lhs[...], rhs[...], preferred_element_type=jnp.float32)
-    for c in sent[:7]:
-        c.wait_recv()
-    mom = mom_box[0]
-    for o in range(1, 8):
-        mom = mom + mom_box[o]
-    finish(mom, 4 * sx, 16 * x, SCALE, chan, acc, zbuf, part1)
-
-    hops = []
-    for o in range(1, 8):
-        g = step(b, o)
-        c = copy(part1.at[g], got1.at[o], 3, o, b_dev(g, y))
-        c.start()
-        hops.append(c)
-    for c in boxes:
-        c.wait_recv()
-    for half in range(2):
-        joined = jnp.zeros((8, 128), jnp.float32)
-        for o in range(8):
-            source = lax.rem(b + 8 - o, 8)
-            joined = joined + jnp.where(source // 4 == half, term_box[o], 0.0)
-        term_all[z, half] = joined
-    sent += boxes
-    boxes = []
-    for o in range(1, 8):
-        c = copy(term_all.at[z], term_all.at[z], 2, o, z_dev(step(z, o)))
-        c.start()
-        boxes.append(c)
-    total = part1[b]
+    total = part1[pl.ds(pl.multiple_of(40 * b, 8), 40), :]
     for c in hops:
         c.wait_recv()
     for o in range(1, 8):
@@ -505,13 +523,14 @@
             pltpu.VMEM((2, 512, 128), f32),
             pltpu.VMEM((3, 16), i32),
             pltpu.SMEM((2, 16), i32),
+            pltpu.SMEM((32,), i32),
             pltpu.VMEM((2, 2, 24), i32),
             pltpu.VMEM((2, 24), f32),
             pltpu.SMEM((2,), i32),
             pltpu.VMEM((8, 8, 128), f32),
             pltpu.VMEM((8, 8, 128), f32),
             pltpu.VMEM((8, 2, 8, 128), f32),
-            pltpu.VMEM((8, 40, 128), f32),
+            pltpu.VMEM((320, 128), f32),
             pltpu.VMEM((8, 40, 128), f32),
             pltpu.VMEM((40, 128), f32),
             pltpu.VMEM((8, 24, 128), f32),

time: 38.4 us -> 37.9 us (0.987)
  Pallas kernels: 37.7 us -> 37.1 us
    pallas_call x1, Pallas kernels: 37 us -> 36.5 us  [local(): pl.pallas_call(kernel, out_shape=(pltpu.VMEM((16, 54), f32), pltpu.VMEM((...]
where the time goes in v4:
time: 37.9 us; the launch traced here: 37.8 us
  Pallas kernels  37.1 us (98%)
  between operations  0.64 us (2%)
    pallas_call x1, Pallas kernels, local(): pl.pallas_call(kernel, out_shape=(pltpu.VMEM((16, 54), f32), pltpu.VMEM((...  36.5 us

profile of v4, /device:TPU:1, one launch (start us, length us, event | category | flops | bytes accessed | tf_op | source)
XLA Modules:
  0.0 37.8 jit_solution(1116877906574809796)
XLA Ops:
  0.6 36.5 %shard_map.77 = (f32[16,54]{1,0:T(8,128)S(1)}, f32[2,2]{1,0:T(2,128)S(1)}) custom-call(bf16[2,12,12,4,1536]{4,3,2,1,0:T(4,128)(2,1)} %s_hbm.1, s32[3,16]{1,0:T(4,128)} %bitcast.2, s32[2,16]{1,0:T(2,128)} %bitcast.3, s32[2,2,24]{2,1,0:T(2,128)} %tindex_hbm.1, f32[2,24]{1,0:T(2,128)} %tweight_hbm.1, s32[2]{0:T(128)} %lengths_hbm.1), custom_call_target="tpu_custom_call" | custom-call | tf_op jit(solution)/shard_map/pallas_call | solution.py:507
  37.1 0.6 %shard_map.78 = (f32[16,54]{1,0:T(8,128)}, f32[2,2]{1,0:T(2,128)}) custom-call(f32[16,54]{1,0:T(8,128)S(1)} %get-tuple-element.4.block, f32[2,2]{1,0:T(2,128)S(1)} %get-tuple-element.5.value), custom_call_target="tpu_custom_call" | custom-call | tf_op jit(solution)/shard_map/pallas_call | solution.py:549

commit v5 on v4

--- a/solution.py
+++ b/solution.py
@@ -323,7 +323,7 @@
 
     pl.semaphore_wait(barrier, jnp.where(alone, 28, 29))
     sent = []
-    for o in range(1, 8):
+    for o in FAR:
         c = copy(mom_box.at[0], mom_box.at[o], 0, o, y_dev(step(y, o)))
         c.start()
         sent.append(c)
@@ -359,7 +359,7 @@
         for o in range(8):
             source = lax.rem(b + 8 - o, 8)
             joined = joined + jnp.where(source // 4 == half, term_box[o], 0.0)
-        term_all[z, half] = joined
+        term_all[z, half] = joined[0:6]
     sent += boxes
     boxes = []
     for o in range(1, 8):
@@ -529,7 +529,7 @@
             pltpu.SMEM((2,), i32),
             pltpu.VMEM((8, 8, 128), f32),
             pltpu.VMEM((8, 8, 128), f32),
-            pltpu.VMEM((8, 2, 8, 128), f32),
+            pltpu.VMEM((8, 2, 6, 128), f32),
             pltpu.VMEM((320, 128), f32),
             pltpu.VMEM((8, 40, 128), f32),
             pltpu.VMEM((40, 128), f32),

time: 37.9 us -> 37.9 us (level)
  no operation moved by 1% of the time
where the time goes in v5:
time: 37.9 us; the launch traced here: 37.7 us
  Pallas kernels  37.1 us (98%)
  between operations  0.64 us (2%)
    pallas_call x1, Pallas kernels, local(): pl.pallas_call(kernel, out_shape=(pltpu.VMEM((16, 54), f32), pltpu.VMEM((...  36.5 us

profile of v5, /device:TPU:1, one launch (start us, length us, event | category | flops | bytes accessed | tf_op | source)
XLA Modules:
  0.0 37.7 jit_solution(104074017639953916)
XLA Ops:
  0.6 36.5 %shard_map.77 = (f32[16,54]{1,0:T(8,128)S(1)}, f32[2,2]{1,0:T(2,128)S(1)}) custom-call(bf16[2,12,12,4,1536]{4,3,2,1,0:T(4,128)(2,1)} %s_hbm.1, s32[3,16]{1,0:T(4,128)} %bitcast.2, s32[2,16]{1,0:T(2,128)} %bitcast.3, s32[2,2,24]{2,1,0:T(2,128)} %tindex_hbm.1, f32[2,24]{1,0:T(2,128)} %tweight_hbm.1, s32[2]{0:T(128)} %lengths_hbm.1), custom_call_target="tpu_custom_call" | custom-call | tf_op jit(solution)/shard_map/pallas_call | solution.py:507
  37.1 0.6 %shard_map.78 = (f32[16,54]{1,0:T(8,128)}, f32[2,2]{1,0:T(2,128)}) custom-call(f32[16,54]{1,0:T(8,128)S(1)} %get-tuple-element.4.block, f32[2,2]{1,0:T(2,128)S(1)} %get-tuple-element.5.value), custom_call_target="tpu_custom_call" | custom-call | tf_op jit(solution)/shard_map/pallas_call | solution.py:549
